TPU v7x, 32 devices: a whole 2x2x4 slice. The times are simulated.
32 devices in a mesh: rows: 8 (over z, x), vox: 4 (over y, core).
Axes of the slice: x: 2, y: 2, z: 4, core: 2. Of those that a mesh axis runs over, the one named last changes fastest.
Arguments:
- system: float32 [1024, 65536], P('rows', 'vox'), may hold values from -0.0234375 to 0.0234375
- measured: float32 [64, 1024], P(None, 'rows'), may hold values from -18 to 18
- start_image: float32 [64, 65536], P('rows', 'vox'), may hold values from 0 to 1
Outputs:
- image: float32 [64, 65536], P('rows', 'vox')
All inputs are finite; a program needn't handle non-finite values.
Results may differ from a plain program's by a relative error of at most 0.0003.
Values sent between devices are 32-bit elements; how exact they have to be, the bound alone decides.
A program may use at most 64 MiB of HBM per device.

v0:
```python
import jax
import jax.numpy as jnp
from jax import lax
from jax.sharding import PartitionSpec as P

lower_bound = 0.0
upper_bound = 1.0


def shifted(block, axis, distance):
    devices = range(lax.axis_size(axis))
    route = [((i - distance) % len(devices), i) for i in devices]
    return lax.ppermute(block, axis, route)


def block_product(current, matrix_tile):
    return lax.dot_general(
        current, matrix_tile, (((1,), (1,)), ((), ())), precision=lax.Precision.HIGHEST
    )


def correct(current, matrix_tile, wanted, summed):
    residual = wanted - summed
    update = jnp.dot(residual, matrix_tile, precision=lax.Precision.HIGHEST)
    return jnp.clip(current + update, lower_bound, upper_bound)


def process(current, matrix_tile, wanted):
    summed = lax.psum(block_product(current, matrix_tile), "vox")
    return correct(current, matrix_tile, wanted, summed)


def shards(system, measured, start_image):
    cycle_size = lax.axis_size("rows")
    position = lax.axis_index("rows")
    frames = start_image.shape[0]

    def visit_image(tick_index, current):
        owner_front = (position - tick_index) % cycle_size
        wanted = lax.dynamic_slice_in_dim(measured, owner_front * frames, frames, 0)
        updated = process(current, system, wanted)
        return shifted(updated, "rows", 1)

    return lax.fori_loop(0, cycle_size, visit_image, start_image)


def solution(mesh):
    placed = (P("rows", "vox"), P(None, "rows"), P("rows", "vox"))
    return jax.shard_map(
        shards, mesh=mesh, in_specs=placed, out_specs=P("rows", "vox"), check_vma=False
    )
```

profile of v0, /device:TPU:0, one launch (start us, length us, event | category | flops | bytes accessed | tf_op | source)
XLA Modules:
  0.0 302.2 jit_solution(4569768256449305872)
XLA Ops:
  0.0 1.0 copy.12
  1.0 300.3 %while.15 = (s32[]{:T(128)}, f32[8,16384]{1,0:T(8,128)S(1)}, s32[]{:T(128)}, f32[64,128]{1,0:T(8,128)}, f32[128,16384]{1,0:T(8,128)}, /*index=5*/s32[]{:T(128)}, s32[]{:T(128)}, s32[]{:T(128)}, s32[]{:T(128)}, s32[]{:T(128)}) while((s32[]{:T(128)}, f32[8,16384]{1,0:T(8,128)S(1)}, s32[]{:T(128)}, f32[64,128]{1,0:T(8,128)}, ...), condition=%wide.region_2.3_spmd, body=%wide.region_0.2_spmd.sunk | while | flops 402917376 | bytes 20468024 | solution.py:44
  1.0 8.9 %fusion.18 = f32[8,128]{1,0:T(8,128)S(1)} fusion(f32[8,16384]{1,0:T(8,128)S(1)} %get-tuple-element.191, f32[128,16384]{1,0:T(8,128)} %get-tuple-element.204), kind=kOutput, calls=%fused_computation.5.clone.1 | convolution fusion | flops 201326592 | bytes 8916992 | tf_op jit(solution)/shard_map/while/body/eval_jaxpr/dot_general | solution.py:17
  9.9 8.4 %psum.15 = f32[8,128]{1,0:T(8,128)S(1)} all-reduce(f32[8,128]{1,0:T(8,128)S(1)} %fusion.18), channel_id=1, replica_groups=mesh['rows'=8,'vox'=4] {'vox'}, use_global_device_ids=true, to_apply=%region_1.1 | all-reduce | flops 1024 | bytes 8192 | tf_op jit(solution)/shard_map/while/body/eval_jaxpr/psum | solution.py:29
  18.3 6.4 %fusion.19 = f32[8,16384]{1,0:T(8,128)S(1)} fusion(f32[8,16384]{1,0:T(8,128)S(1)} %get-tuple-element.191, f32[128,16384]{1,0:T(8,128)} %get-tuple-element.204, f32[8,128]{1,0:T(8,128)S(1)} %psum.15, f32[64,128]{1,0:T(8,128)} %get-tuple-element.203, s32[]{:T(128)S(6)} %select_n.33), kind=kOutput, calls=%fused_computation.1.clone.1 | convolution fusion | flops 201589760 | bytes 9445380 | tf_op jit(solution)/shard_map/while/body/eval_jaxpr/dot_general | solution.py:24
  24.7 1.5 collective-permute-start
  26.2 13.7 %collective-permute-done = f32[8,16384]{1,0:T(8,128)S(1)} collective-permute-done((f32[8,16384]{1,0:T(8,128)S(1)}, f32[8,16384]{1,0:T(8,128)S(1)}, u32[]{:S(2)}, u32[]{:S(2)}) %collective-permute-start) | collective-permute-done | bytes 524320 | tf_op jit(solution)/shard_map/while/body/eval_jaxpr/ppermute | solution.py:13
  39.9 8.9 %fusion.18 = f32[8,128]{1,0:T(8,128)S(1)} fusion(f32[8,16384]{1,0:T(8,128)S(1)} %get-tuple-element.191, f32[128,16384]{1,0:T(8,128)} %get-tuple-element.204), kind=kOutput, calls=%fused_computation.5.clone.1 | convolution fusion | flops 201326592 | bytes 8916992 | tf_op jit(solution)/shard_map/while/body/eval_jaxpr/dot_general | solution.py:17
  48.8 5.8 %psum.15 = f32[8,128]{1,0:T(8,128)S(1)} all-reduce(f32[8,128]{1,0:T(8,128)S(1)} %fusion.18), channel_id=1, replica_groups=mesh['rows'=8,'vox'=4] {'vox'}, use_global_device_ids=true, to_apply=%region_1.1 | all-reduce | flops 1024 | bytes 8192 | tf_op jit(solution)/shard_map/while/body/eval_jaxpr/psum | solution.py:29
  54.6 6.4 %fusion.19 = f32[8,16384]{1,0:T(8,128)S(1)} fusion(f32[8,16384]{1,0:T(8,128)S(1)} %get-tuple-element.191, f32[128,16384]{1,0:T(8,128)} %get-tuple-element.204, f32[8,128]{1,0:T(8,128)S(1)} %psum.15, f32[64,128]{1,0:T(8,128)} %get-tuple-element.203, s32[]{:T(128)S(6)} %select_n.33), kind=kOutput, calls=%fused_computation.1.clone.1 | convolution fusion | flops 201589760 | bytes 9445380 | tf_op jit(solution)/shard_map/while/body/eval_jaxpr/dot_general | solution.py:24
  61.0 0.1 collective-permute-start
  61.1 16.2 %collective-permute-done = f32[8,16384]{1,0:T(8,128)S(1)} collective-permute-done((f32[8,16384]{1,0:T(8,128)S(1)}, f32[8,16384]{1,0:T(8,128)S(1)}, u32[]{:S(2)}, u32[]{:S(2)}) %collective-permute-start) | collective-permute-done | bytes 524320 | tf_op jit(solution)/shard_map/while/body/eval_jaxpr/ppermute | solution.py:13
  77.3 8.9 %fusion.18 = f32[8,128]{1,0:T(8,128)S(1)} fusion(f32[8,16384]{1,0:T(8,128)S(1)} %get-tuple-element.191, f32[128,16384]{1,0:T(8,128)} %get-tuple-element.204), kind=kOutput, calls=%fused_computation.5.clone.1 | convolution fusion | flops 201326592 | bytes 8916992 | tf_op jit(solution)/shard_map/while/body/eval_jaxpr/dot_general | solution.py:17
  86.2 5.7 %psum.15 = f32[8,128]{1,0:T(8,128)S(1)} all-reduce(f32[8,128]{1,0:T(8,128)S(1)} %fusion.18), channel_id=1, replica_groups=mesh['rows'=8,'vox'=4] {'vox'}, use_global_device_ids=true, to_apply=%region_1.1 | all-reduce | flops 1024 | bytes 8192 | tf_op jit(solution)/shard_map/while/body/eval_jaxpr/psum | solution.py:29
  91.8 6.4 %fusion.19 = f32[8,16384]{1,0:T(8,128)S(1)} fusion(f32[8,16384]{1,0:T(8,128)S(1)} %get-tuple-element.191, f32[128,16384]{1,0:T(8,128)} %get-tuple-element.204, f32[8,128]{1,0:T(8,128)S(1)} %psum.15, f32[64,128]{1,0:T(8,128)} %get-tuple-element.203, s32[]{:T(128)S(6)} %select_n.33), kind=kOutput, calls=%fused_computation.1.clone.1 | convolution fusion | flops 201589760 | bytes 9445380 | tf_op jit(solution)/shard_map/while/body/eval_jaxpr/dot_general | solution.py:24
  98.2 0.1 collective-permute-start
  98.3 16.4 %collective-permute-done = f32[8,16384]{1,0:T(8,128)S(1)} collective-permute-done((f32[8,16384]{1,0:T(8,128)S(1)}, f32[8,16384]{1,0:T(8,128)S(1)}, u32[]{:S(2)}, u32[]{:S(2)}) %collective-permute-start) | collective-permute-done | bytes 524320 | tf_op jit(solution)/shard_map/while/body/eval_jaxpr/ppermute | solution.py:13
  114.6 8.9 %fusion.18 = f32[8,128]{1,0:T(8,128)S(1)} fusion(f32[8,16384]{1,0:T(8,128)S(1)} %get-tuple-element.191, f32[128,16384]{1,0:T(8,128)} %get-tuple-element.204), kind=kOutput, calls=%fused_computation.5.clone.1 | convolution fusion | flops 201326592 | bytes 8916992 | tf_op jit(solution)/shard_map/while/body/eval_jaxpr/dot_general | solution.py:17
  123.5 5.7 %psum.15 = f32[8,128]{1,0:T(8,128)S(1)} all-reduce(f32[8,128]{1,0:T(8,128)S(1)} %fusion.18), channel_id=1, replica_groups=mesh['rows'=8,'vox'=4] {'vox'}, use_global_device_ids=true, to_apply=%region_1.1 | all-reduce | flops 1024 | bytes 8192 | tf_op jit(solution)/shard_map/while/body/eval_jaxpr/psum | solution.py:29
  129.2 6.4 %fusion.19 = f32[8,16384]{1,0:T(8,128)S(1)} fusion(f32[8,16384]{1,0:T(8,128)S(1)} %get-tuple-element.191, f32[128,16384]{1,0:T(8,128)} %get-tuple-element.204, f32[8,128]{1,0:T(8,128)S(1)} %psum.15, f32[64,128]{1,0:T(8,128)} %get-tuple-element.203, s32[]{:T(128)S(6)} %select_n.33), kind=kOutput, calls=%fused_computation.1.clone.1 | convolution fusion | flops 201589760 | bytes 9445380 | tf_op jit(solution)/shard_map/while/body/eval_jaxpr/dot_general | solution.py:24
  135.5 0.1 collective-permute-start
  135.6 16.4 %collective-permute-done = f32[8,16384]{1,0:T(8,128)S(1)} collective-permute-done((f32[8,16384]{1,0:T(8,128)S(1)}, f32[8,16384]{1,0:T(8,128)S(1)}, u32[]{:S(2)}, u32[]{:S(2)}) %collective-permute-start) | collective-permute-done | bytes 524320 | tf_op jit(solution)/shard_map/while/body/eval_jaxpr/ppermute | solution.py:13
  152.0 8.9 %fusion.18 = f32[8,128]{1,0:T(8,128)S(1)} fusion(f32[8,16384]{1,0:T(8,128)S(1)} %get-tuple-element.191, f32[128,16384]{1,0:T(8,128)} %get-tuple-element.204), kind=kOutput, calls=%fused_computation.5.clone.1 | convolution fusion | flops 201326592 | bytes 8916992 | tf_op jit(solution)/shard_map/while/body/eval_jaxpr/dot_general | solution.py:17
  160.9 5.7 %psum.15 = f32[8,128]{1,0:T(8,128)S(1)} all-reduce(f32[8,128]{1,0:T(8,128)S(1)} %fusion.18), channel_id=1, replica_groups=mesh['rows'=8,'vox'=4] {'vox'}, use_global_device_ids=true, to_apply=%region_1.1 | all-reduce | flops 1024 | bytes 8192 | tf_op jit(solution)/shard_map/while/body/eval_jaxpr/psum | solution.py:29
  166.5 6.4 %fusion.19 = f32[8,16384]{1,0:T(8,128)S(1)} fusion(f32[8,16384]{1,0:T(8,128)S(1)} %get-tuple-element.191, f32[128,16384]{1,0:T(8,128)} %get-tuple-element.204, f32[8,128]{1,0:T(8,128)S(1)} %psum.15, f32[64,128]{1,0:T(8,128)} %get-tuple-element.203, s32[]{:T(128)S(6)} %select_n.33), kind=kOutput, calls=%fused_computation.1.clone.1 | convolution fusion | flops 201589760 | bytes 9445380 | tf_op jit(solution)/shard_map/while/body/eval_jaxpr/dot_general | solution.py:24
  172.9 0.1 collective-permute-start
  173.0 16.4 %collective-permute-done = f32[8,16384]{1,0:T(8,128)S(1)} collective-permute-done((f32[8,16384]{1,0:T(8,128)S(1)}, f32[8,16384]{1,0:T(8,128)S(1)}, u32[]{:S(2)}, u32[]{:S(2)}) %collective-permute-start) | collective-permute-done | bytes 524320 | tf_op jit(solution)/shard_map/while/body/eval_jaxpr/ppermute | solution.py:13
  189.3 8.9 %fusion.18 = f32[8,128]{1,0:T(8,128)S(1)} fusion(f32[8,16384]{1,0:T(8,128)S(1)} %get-tuple-element.191, f32[128,16384]{1,0:T(8,128)} %get-tuple-element.204), kind=kOutput, calls=%fused_computation.5.clone.1 | convolution fusion | flops 201326592 | bytes 8916992 | tf_op jit(solution)/shard_map/while/body/eval_jaxpr/dot_general | solution.py:17
  198.2 5.7 %psum.15 = f32[8,128]{1,0:T(8,128)S(1)} all-reduce(f32[8,128]{1,0:T(8,128)S(1)} %fusion.18), channel_id=1, replica_groups=mesh['rows'=8,'vox'=4] {'vox'}, use_global_device_ids=true, to_apply=%region_1.1 | all-reduce | flops 1024 | bytes 8192 | tf_op jit(solution)/shard_map/while/body/eval_jaxpr/psum | solution.py:29
  203.9 6.4 %fusion.19 = f32[8,16384]{1,0:T(8,128)S(1)} fusion(f32[8,16384]{1,0:T(8,128)S(1)} %get-tuple-element.191, f32[128,16384]{1,0:T(8,128)} %get-tuple-element.204, f32[8,128]{1,0:T(8,128)S(1)} %psum.15, f32[64,128]{1,0:T(8,128)} %get-tuple-element.203, s32[]{:T(128)S(6)} %select_n.33), kind=kOutput, calls=%fused_computation.1.clone.1 | convolution fusion | flops 201589760 | bytes 9445380 | tf_op jit(solution)/shard_map/while/body/eval_jaxpr/dot_general | solution.py:24
  210.2 0.1 collective-permute-start
  210.3 16.4 %collective-permute-done = f32[8,16384]{1,0:T(8,128)S(1)} collective-permute-done((f32[8,16384]{1,0:T(8,128)S(1)}, f32[8,16384]{1,0:T(8,128)S(1)}, u32[]{:S(2)}, u32[]{:S(2)}) %collective-permute-start) | collective-permute-done | bytes 524320 | tf_op jit(solution)/shard_map/while/body/eval_jaxpr/ppermute | solution.py:13
  226.7 8.9 %fusion.18 = f32[8,128]{1,0:T(8,128)S(1)} fusion(f32[8,16384]{1,0:T(8,128)S(1)} %get-tuple-element.191, f32[128,16384]{1,0:T(8,128)} %get-tuple-element.204), kind=kOutput, calls=%fused_computation.5.clone.1 | convolution fusion | flops 201326592 | bytes 8916992 | tf_op jit(solution)/shard_map/while/body/eval_jaxpr/dot_general | solution.py:17
  235.6 5.7 %psum.15 = f32[8,128]{1,0:T(8,128)S(1)} all-reduce(f32[8,128]{1,0:T(8,128)S(1)} %fusion.18), channel_id=1, replica_groups=mesh['rows'=8,'vox'=4] {'vox'}, use_global_device_ids=true, to_apply=%region_1.1 | all-reduce | flops 1024 | bytes 8192 | tf_op jit(solution)/shard_map/while/body/eval_jaxpr/psum | solution.py:29
  241.2 6.4 %fusion.19 = f32[8,16384]{1,0:T(8,128)S(1)} fusion(f32[8,16384]{1,0:T(8,128)S(1)} %get-tuple-element.191, f32[128,16384]{1,0:T(8,128)} %get-tuple-element.204, f32[8,128]{1,0:T(8,128)S(1)} %psum.15, f32[64,128]{1,0:T(8,128)} %get-tuple-element.203, s32[]{:T(128)S(6)} %select_n.33), kind=kOutput, calls=%fused_computation.1.clone.1 | convolution fusion | flops 201589760 | bytes 9445380 | tf_op jit(solution)/shard_map/while/body/eval_jaxpr/dot_general | solution.py:24
  247.6 0.1 collective-permute-start
  247.7 16.4 %collective-permute-done = f32[8,16384]{1,0:T(8,128)S(1)} collective-permute-done((f32[8,16384]{1,0:T(8,128)S(1)}, f32[8,16384]{1,0:T(8,128)S(1)}, u32[]{:S(2)}, u32[]{:S(2)}) %collective-permute-start) | collective-permute-done | bytes 524320 | tf_op jit(solution)/shard_map/while/body/eval_jaxpr/ppermute | solution.py:13
  264.0 8.9 %fusion.18 = f32[8,128]{1,0:T(8,128)S(1)} fusion(f32[8,16384]{1,0:T(8,128)S(1)} %get-tuple-element.191, f32[128,16384]{1,0:T(8,128)} %get-tuple-element.204), kind=kOutput, calls=%fused_computation.5.clone.1 | convolution fusion | flops 201326592 | bytes 8916992 | tf_op jit(solution)/shard_map/while/body/eval_jaxpr/dot_general | solution.py:17
  272.9 5.7 %psum.15 = f32[8,128]{1,0:T(8,128)S(1)} all-reduce(f32[8,128]{1,0:T(8,128)S(1)} %fusion.18), channel_id=1, replica_groups=mesh['rows'=8,'vox'=4] {'vox'}, use_global_device_ids=true, to_apply=%region_1.1 | all-reduce | flops 1024 | bytes 8192 | tf_op jit(solution)/shard_map/while/body/eval_jaxpr/psum | solution.py:29
  278.6 6.4 %fusion.19 = f32[8,16384]{1,0:T(8,128)S(1)} fusion(f32[8,16384]{1,0:T(8,128)S(1)} %get-tuple-element.191, f32[128,16384]{1,0:T(8,128)} %get-tuple-element.204, f32[8,128]{1,0:T(8,128)S(1)} %psum.15, f32[64,128]{1,0:T(8,128)} %get-tuple-element.203, s32[]{:T(128)S(6)} %select_n.33), kind=kOutput, calls=%fused_computation.1.clone.1 | convolution fusion | flops 201589760 | bytes 9445380 | tf_op jit(solution)/shard_map/while/body/eval_jaxpr/dot_general | solution.py:24
  285.0 0.1 collective-permute-start
  285.0 16.3 %collective-permute-done = f32[8,16384]{1,0:T(8,128)S(1)} collective-permute-done((f32[8,16384]{1,0:T(8,128)S(1)}, f32[8,16384]{1,0:T(8,128)S(1)}, u32[]{:S(2)}, u32[]{:S(2)}) %collective-permute-start) | collective-permute-done | bytes 524320 | tf_op jit(solution)/shard_map/while/body/eval_jaxpr/ppermute | solution.py:13
  301.4 0.8 copy.13
Async XLA Ops:
  24.7 15.3 %collective-permute-start = (f32[8,16384]{1,0:T(8,128)S(1)}, f32[8,16384]{1,0:T(8,128)S(1)}, u32[]{:S(2)}, u32[]{:S(2)}) collective-permute-start(f32[8,16384]{1,0:T(8,128)S(1)} %fusion.19), channel_id=1, source_target_pairs={{28,0},{0,4},{4,8},{8,12},{12,16},{16,20},{20,24},{24,28},{29,1},{... | collective-permute-start | bytes 1572872 | tf_op jit(solution)/shard_map/while/body/eval_jaxpr/ppermute | solution.py:13
  61.0 16.3 %collective-permute-start = (f32[8,16384]{1,0:T(8,128)S(1)}, f32[8,16384]{1,0:T(8,128)S(1)}, u32[]{:S(2)}, u32[]{:S(2)}) collective-permute-start(f32[8,16384]{1,0:T(8,128)S(1)} %fusion.19), channel_id=1, source_target_pairs={{28,0},{0,4},{4,8},{8,12},{12,16},{16,20},{20,24},{24,28},{29,1},{... | collective-permute-start | bytes 1572872 | tf_op jit(solution)/shard_map/while/body/eval_jaxpr/ppermute | solution.py:13
  98.2 16.4 %collective-permute-start = (f32[8,16384]{1,0:T(8,128)S(1)}, f32[8,16384]{1,0:T(8,128)S(1)}, u32[]{:S(2)}, u32[]{:S(2)}) collective-permute-start(f32[8,16384]{1,0:T(8,128)S(1)} %fusion.19), channel_id=1, source_target_pairs={{28,0},{0,4},{4,8},{8,12},{12,16},{16,20},{20,24},{24,28},{29,1},{... | collective-permute-start | bytes 1572872 | tf_op jit(solution)/shard_map/while/body/eval_jaxpr/ppermute | solution.py:13
  135.5 16.4 %collective-permute-start = (f32[8,16384]{1,0:T(8,128)S(1)}, f32[8,16384]{1,0:T(8,128)S(1)}, u32[]{:S(2)}, u32[]{:S(2)}) collective-permute-start(f32[8,16384]{1,0:T(8,128)S(1)} %fusion.19), channel_id=1, source_target_pairs={{28,0},{0,4},{4,8},{8,12},{12,16},{16,20},{20,24},{24,28},{29,1},{... | collective-permute-start | bytes 1572872 | tf_op jit(solution)/shard_map/while/body/eval_jaxpr/ppermute | solution.py:13
  172.9 16.4 %collective-permute-start = (f32[8,16384]{1,0:T(8,128)S(1)}, f32[8,16384]{1,0:T(8,128)S(1)}, u32[]{:S(2)}, u32[]{:S(2)}) collective-permute-start(f32[8,16384]{1,0:T(8,128)S(1)} %fusion.19), channel_id=1, source_target_pairs={{28,0},{0,4},{4,8},{8,12},{12,16},{16,20},{20,24},{24,28},{29,1},{... | collective-permute-start | bytes 1572872 | tf_op jit(solution)/shard_map/while/body/eval_jaxpr/ppermute | solution.py:13
  210.2 16.4 %collective-permute-start = (f32[8,16384]{1,0:T(8,128)S(1)}, f32[8,16384]{1,0:T(8,128)S(1)}, u32[]{:S(2)}, u32[]{:S(2)}) collective-permute-start(f32[8,16384]{1,0:T(8,128)S(1)} %fusion.19), channel_id=1, source_target_pairs={{28,0},{0,4},{4,8},{8,12},{12,16},{16,20},{20,24},{24,28},{29,1},{... | collective-permute-start | bytes 1572872 | tf_op jit(solution)/shard_map/while/body/eval_jaxpr/ppermute | solution.py:13
  247.6 16.4 %collective-permute-start = (f32[8,16384]{1,0:T(8,128)S(1)}, f32[8,16384]{1,0:T(8,128)S(1)}, u32[]{:S(2)}, u32[]{:S(2)}) collective-permute-start(f32[8,16384]{1,0:T(8,128)S(1)} %fusion.19), channel_id=1, source_target_pairs={{28,0},{0,4},{4,8},{8,12},{12,16},{16,20},{20,24},{24,28},{29,1},{... | collective-permute-start | bytes 1572872 | tf_op jit(solution)/shard_map/while/body/eval_jaxpr/ppermute | solution.py:13
  285.0 16.4 %collective-permute-start = (f32[8,16384]{1,0:T(8,128)S(1)}, f32[8,16384]{1,0:T(8,128)S(1)}, u32[]{:S(2)}, u32[]{:S(2)}) collective-permute-start(f32[8,16384]{1,0:T(8,128)S(1)} %fusion.19), channel_id=1, source_target_pairs={{28,0},{0,4},{4,8},{8,12},{12,16},{16,20},{20,24},{24,28},{29,1},{... | collective-permute-start | bytes 1572872 | tf_op jit(solution)/shard_map/while/body/eval_jaxpr/ppermute | solution.py:13
where the time goes:
time: 303 us; the launch traced here: 302 us
  waiting for transfers between devices  128 us (42%)
  matrix products  122 us (40%)
  blocking collectives  48.2 us (16%)
    ppermute x8, waiting for transfers between devices, shifted(): return lax.ppermute(block, axis, route)  128 us
    dot_general x8, matrix products, block_product(): lax.dot_general(current, matrix_tile, (((1,), (1,)), ((), ())), precision...  71 us
    dot_general x8, matrix products, correct(): update = jnp.dot(residual, matrix_tile, precision=lax.Precision.HIGHEST)  50.9 us
    psum x8, blocking collectives, process(): summed = lax.psum(block_product(current, matrix_tile), 'vox')  48.2 us
  transfers between devices with their start and end apart: 8, of which 8 were waited for; matrix products, arithmetic and copies ran while one was open for 0% of the time, Pallas kernels for 0%

commit v1 on v0

v1 whole, which is shorter than its diff:
```python
import functools

import jax
import jax.numpy as jnp
from jax import lax
from jax.experimental import pallas as pl
from jax.experimental.pallas import tpu as pltpu
from jax.sharding import PartitionSpec as P

lower_bound = 0.0
upper_bound = 1.0
HALVES = 2
CHUNKS = 8
EARLY = 5


def split(value):
    high = value.astype(jnp.bfloat16).astype(jnp.float32)
    return high, value - high


def fold(product, rows, cols):
    by_row = product[:rows] + product[rows:]
    return by_row[:, :cols] + by_row[:, cols:]


def kernel(
    cycle, peers, system, measured, start, out,
    landed, tiles, staged, slots, shares, total,
    load_sem, x_sem, sent_sem, got_sem, share_sent, share_got,
):
    me = lax.axis_index("rows")
    mine = lax.axis_index("vox")
    right = lax.rem(me + 1, cycle)
    left = lax.rem(me + cycle - 1, cycle)
    block_rows, voxels = system.shape
    frames = start.shape[0]
    half = frames // HALVES
    width = voxels // CHUNKS
    steps = cycle * HALVES

    def cut(c):
        return pl.ds(c * width, width)

    def load(c):
        return pltpu.make_async_copy(
            system.at[:, cut(c)], landed.at[:, cut(c)], load_sem.at[c]
        )

    fetch = pltpu.make_async_copy(start, staged, x_sem)
    fetch.start()
    for c in range(CHUNKS):
        load(c).start()

    barrier = pltpu.get_barrier_semaphore()
    for neighbour in (left, right):
        pl.semaphore_signal(barrier, inc=1, device_id={"rows": neighbour})
    for away in range(1, peers):
        pl.semaphore_signal(
            barrier, inc=1, device_id={"vox": lax.rem(mine + away, peers)}
        )

    def share_copy(h, away):
        return pltpu.make_async_remote_copy(
            src_ref=shares.at[h, mine],
            dst_ref=shares.at[h, mine],
            send_sem=share_sent.at[h],
            recv_sem=share_got.at[h, mine],
            device_id={"vox": lax.rem(mine + away, peers)},
        )

    def send_share(h, product):
        shares[h, mine] = product
        for away in range(1, peers):
            share_copy(h, away).start()

    def image_copy(h, c):
        return pltpu.make_async_remote_copy(
            src_ref=slots.at[h, :, cut(c)],
            dst_ref=slots.at[h + HALVES, :, cut(c)],
            send_sem=sent_sem.at[h],
            recv_sem=got_sem.at[h + HALVES, c],
            device_id={"rows": right},
        )

    def wait_image(h, c):
        piece = slots.at[h, :, cut(c)]
        pltpu.make_async_copy(piece, piece, got_sem.at[h, c]).wait()

    def wait_sent(h):
        whole = slots.at[h]
        pltpu.make_async_copy(whole, whole, sent_sem.at[h]).wait()
        several = shares.at[h, pl.ds(0, peers - 1)]
        pltpu.make_async_copy(several, several, share_sent.at[h]).wait()

    def stacked(value):
        return jnp.concatenate(split(value), axis=0).astype(jnp.bfloat16)

    def times_tiles(value, c):
        return lax.dot_general(
            stacked(value), tiles[:, cut(c)], (((1,), (1,)), ((), ())),
            preferred_element_type=jnp.float32,
        )

    fetch.wait()
    first = jnp.zeros((2 * frames, 2 * block_rows), jnp.float32)
    for c in range(CHUNKS):
        load(c).wait()
        high, low = split(landed[:, cut(c)])
        tiles[pl.ds(0, block_rows), cut(c)] = high.astype(jnp.bfloat16)
        tiles[pl.ds(block_rows, block_rows), cut(c)] = low.astype(jnp.bfloat16)
        now = staged[:, cut(c)]
        for s in range(HALVES):
            slots[s, :, cut(c)] = now[s * half:(s + 1) * half]
        first += times_tiles(now, c)
    first = fold(first, frames, block_rows)

    pl.semaphore_wait(barrier, 2 + peers - 1)
    for s in range(HALVES):
        send_share(s, first[s * half:(s + 1) * half])

    def step(h, carry):
        tick = h // HALVES
        part = lax.rem(h, HALVES)
        owner = lax.rem(me - tick + cycle, cycle)
        ahead = jnp.logical_and(h > 0, h < steps - 1)

        @pl.when(ahead)
        def _():
            acc = jnp.zeros(total.shape, jnp.float32)
            for c in range(EARLY):
                wait_image(h + 1, c)
                acc += times_tiles(slots[h + 1, :, cut(c)], c)
            total[...] = acc

        for away in range(1, peers):
            source = lax.rem(mine + away, peers)
            piece = shares.at[h, source]
            pltpu.make_async_copy(piece, piece, share_got.at[h, source]).wait()
        summed = shares[h, 0]
        for v in range(1, peers):
            summed += shares[h, v]
        front = measured[pl.ds(pl.multiple_of(owner * frames, frames), frames), :]
        wanted = front[:half]
        for s in range(1, HALVES):
            wanted = jnp.where(part == s, front[s * half:(s + 1) * half], wanted)
        parts = stacked(wanted - summed)
        twice = jnp.concatenate([parts, parts], axis=1)
        for c in range(CHUNKS):
            update = jnp.dot(
                twice, tiles[:, cut(c)], preferred_element_type=jnp.float32
            )
            update = update[:half] + update[half:]
            slots[h, :, cut(c)] = jnp.clip(
                slots[h, :, cut(c)] + update, lower_bound, upper_bound
            )
            image_copy(h, c).start()

        @pl.when(ahead)
        def _():
            acc = total[...]
            for c in range(EARLY, CHUNKS):
                wait_image(h + 1, c)
                acc += times_tiles(slots[h + 1, :, cut(c)], c)
            send_share(h + 1, fold(acc, half, block_rows))

        @pl.when(h >= HALVES)
        def _():
            wait_sent(h - HALVES)

        return carry

    lax.fori_loop(0, steps, step, 0)

    for s in range(HALVES):
        for c in range(CHUNKS):
            wait_image(steps + s, c)
            out[s * half:(s + 1) * half, cut(c)] = slots[steps + s, :, cut(c)]
    for s in range(HALVES):
        wait_sent(steps - HALVES + s)


def shards(system, measured, start_image):
    cycle = lax.axis_size("rows")
    peers = lax.axis_size("vox")
    block_rows, voxels = system.shape
    frames = start_image.shape[0]
    half = frames // HALVES
    steps = cycle * HALVES
    anywhere = pl.BlockSpec(memory_space=pl.ANY)
    near = pl.BlockSpec(memory_space=pltpu.VMEM)
    dma = pltpu.SemaphoreType.DMA
    return pl.pallas_call(
        functools.partial(kernel, cycle, peers),
        out_shape=jax.ShapeDtypeStruct(start_image.shape, start_image.dtype),
        in_specs=[anywhere, near, anywhere],
        out_specs=near,
        scratch_shapes=[
            pltpu.VMEM((block_rows, voxels), jnp.float32),
            pltpu.VMEM((2 * block_rows, voxels), jnp.bfloat16),
            pltpu.VMEM((frames, voxels), jnp.float32),
            pltpu.VMEM((steps + HALVES, half, voxels), jnp.float32),
            pltpu.VMEM((steps, peers, half, block_rows), jnp.float32),
            pltpu.VMEM((2 * half, 2 * block_rows), jnp.float32),
            dma((CHUNKS,)),
            dma,
            dma((steps,)),
            dma((steps + HALVES, CHUNKS)),
            dma((steps,)),
            dma((steps, peers)),
        ],
        compiler_params=pltpu.CompilerParams(
            collective_id=0, has_side_effects=True, vmem_limit_bytes=56 * 2**20
        ),
    )(system, measured, start_image)


def solution(mesh):
    placed = (P("rows", "vox"), P(None, "rows"), P("rows", "vox"))
    return jax.shard_map(
        shards, mesh=mesh, in_specs=placed, out_specs=P("rows", "vox"), check_vma=False
    )
```

time: 303 us -> 135 us (0.45)
  Pallas kernels: 0 us -> 133 us
  waiting for transfers between devices: 128 us -> 0 us
  matrix products: 122 us -> 0 us
  blocking collectives: 48.2 us -> 0 us
    pallas_call x0 -> x1, Pallas kernels: none -> 133 us  [shards(): pl.pallas_call(functools.partial(kernel, cycle, peers), out_shape=jax.Sha...]
    ppermute x8 -> x0, waiting for transfers between devices: 128 us -> none  [shifted(): return lax.ppermute(block, axis, route)]
    dot_general x16 -> x0, matrix products: 122 us -> none  [the longest x8 71 us: block_product(): lax.dot_general(current, matrix_tile, (((1,), (1,)), ((), ())), precision...]
    psum x8 -> x0, blocking collectives: 48.2 us -> none  [process(): summed = lax.psum(block_product(current, matrix_tile), 'vox')]
  transfers between devices with their start and end apart: 8 -> 0, of which waited for: 8 -> 0; matrix products, arithmetic and copies ran while one was open for 0% -> 0% of each run, Pallas kernels for 0% -> 0%
where the time goes in v1:
time: 135 us
  Pallas kernels  133 us (99%)
  local copies, waits for them, and re-layouts  1.87 us (1%)
    pallas_call x1, Pallas kernels, shards(): pl.pallas_call(functools.partial(kernel, cycle, peers), out_shape=jax.Sha...  133 us

profile of v1, /device:TPU:0, one launch (start us, length us, event | category | flops | bytes accessed | tf_op | source)
XLA Modules:
  0.0 134.7 jit_solution(17830168998321721052)
XLA Ops:
  0.0 132.9 %shard_map.37 = f32[8,16384]{1,0:T(8,128)} custom-call(f32[128,16384]{1,0:T(8,128)} %system.1, f32[64,128]{1,0:T(8,128)} %measured.1, f32[8,16384]{1,0:T(8,128)} %start.1), custom_call_target="tpu_custom_call" | custom-call | tf_op jit(solution)/shard_map/pallas_call | solution.py:193
  132.9 1.9 %copy.5 = f32[8,16384]{1,0:T(8,128)} copy(f32[8,16384]{1,0:T(8,128)} %shard_map.37) | data formatting | bytes 1048576

commit v2 on v1

--- a/solution.py
+++ b/solution.py
@@ -10,8 +10,9 @@
 lower_bound = 0.0
 upper_bound = 1.0
 HALVES = 2
-CHUNKS = 8
-EARLY = 5
+CHUNKS = 4
+EARLY = 2
+LEAD = 4
 
 
 def split(value):
@@ -146,7 +147,7 @@
             wanted = jnp.where(part == s, front[s * half:(s + 1) * half], wanted)
         parts = stacked(wanted - summed)
         twice = jnp.concatenate([parts, parts], axis=1)
-        for c in range(CHUNKS):
+        def visit(c):
             update = jnp.dot(
                 twice, tiles[:, cut(c)], preferred_element_type=jnp.float32
             )
@@ -156,6 +157,9 @@
             )
             image_copy(h, c).start()
 
+        for c in range(LEAD):
+            visit(c)
+
         @pl.when(ahead)
         def _():
             acc = total[...]
@@ -163,6 +167,9 @@
                 wait_image(h + 1, c)
                 acc += times_tiles(slots[h + 1, :, cut(c)], c)
             send_share(h + 1, fold(acc, half, block_rows))
+
+        for c in range(LEAD, CHUNKS):
+            visit(c)
 
         @pl.when(h >= HALVES)
         def _():

time: 135 us -> 135 us (level)
  no operation moved by 1% of the time
where the time goes in v2:
time: 135 us
  Pallas kernels  133 us (99%)
  local copies, waits for them, and re-layouts  1.87 us (1%)
    pallas_call x1, Pallas kernels, shards(): pl.pallas_call(functools.partial(kernel, cycle, peers), out_shape=jax.Sha...  133 us

profile of v2, /device:TPU:0, one launch (start us, length us, event | category | flops | bytes accessed | tf_op | source)
XLA Modules:
  0.0 134.7 jit_solution(873606819065811147)
XLA Ops:
  0.0 132.9 %shard_map.37 = f32[8,16384]{1,0:T(8,128)} custom-call(f32[128,16384]{1,0:T(8,128)} %system.1, f32[64,128]{1,0:T(8,128)} %measured.1, f32[8,16384]{1,0:T(8,128)} %start.1), custom_call_target="tpu_custom_call" | custom-call | tf_op jit(solution)/shard_map/pallas_call | solution.py:200
  132.9 1.9 %copy.5 = f32[8,16384]{1,0:T(8,128)} copy(f32[8,16384]{1,0:T(8,128)} %shard_map.37) | data formatting | bytes 1048576
